TPU v7x, 128 devices: a whole 4x4x4 slice. The times are simulated.
128 devices in a mesh: gx: 8 (over y, core), gy: 16 (over x, z).
Axes of the slice: x: 4, y: 4, z: 4, core: 2. Of those that a mesh axis runs over, the one named last changes fastest.
Arguments:
- load: float32 [8, 16, 2, 112, 512], P('gx', 'gy'), may hold values from -6 to 6
- schur_inv: bfloat16 [8, 16, 2048, 2048], P('gx', 'gy'), as said below
- schur: bfloat16 [8, 16, 2048, 2048], P('gx', 'gy'), as said below
- coupling: bfloat16 [8, 16, 2048, 192], P('gx', 'gy'), may hold values from -0.125 to 0.125
- pairing: int32 [8, 16, 2, 4], P('gx', 'gy'), may hold values from 0 to 3, each once within a row
- corner_rows: int32 [8, 16, 192], P('gx', 'gy'), may hold values from 0 to 12287, as said below
- coarse_inv: float32 [12288, 96], P(('gx', 'gy')), as said below
Outputs:
- multipliers: float32 [8, 16, 2, 112, 512], P('gx', 'gy')
- residual: float32 [8, 16, 2, 112, 512], P('gx', 'gy')
Inputs may be any that keep to these rules, and one draw needn't show every extreme that they name: `schur_inv`: each subdomain's block is symmetric positive definite. `schur`: each subdomain's block is symmetric positive definite. `coarse_inv`: each block of 96 rows is symmetric positive definite. `corner_rows`: of one subdomain's 192 entries at most 3 lie in one block of 96 rows (rows b*96 to (b+1)*96 - 1); one block holds exactly 3 entries of every subdomain.
All inputs are finite; a program needn't handle non-finite values.
Results may differ from a plain program's by a relative error of at most 0.04.
Values may be sent and summed in bfloat16 or wider, within the bound.
A program may use at most 128 MiB of HBM per device.

v0:
```python
import jax
import jax.numpy as jnp
from jax import lax
from jax.sharding import PartitionSpec as P

ITERS = 3


HIGH = lax.Precision.HIGHEST


def passed_along(value, axis, steps):
    count = lax.axis_size(axis)
    first, last = (max(0, -steps), min(count, count - steps))
    return lax.ppermute(value, axis, [(source, source + steps) for source in range(first, last)])


def assemble(field, table_half):
    count_rhs, width = (field.shape[1], field.shape[2])
    groups = table_half.shape[1]
    from_left = passed_along(field[0], "gx", 1)
    from_below = passed_along(field[1], "gy", 1)
    left = jnp.einsum(
        "jk,rkb->rjb",
        table_half[0],
        from_left.reshape(count_rhs, groups, -1),
        preferred_element_type=jnp.float32,
    )
    lower = jnp.einsum(
        "jk,rkb->rjb",
        table_half[1],
        from_below.reshape(count_rhs, groups, -1),
        preferred_element_type=jnp.float32,
    )
    left = left.astype(jnp.bfloat16).reshape(count_rhs, width)
    lower = lower.astype(jnp.bfloat16).reshape(count_rhs, width)
    return jnp.concatenate([-left, field[0], -lower, field[1]], axis=-1)


def jump(values, table, live):
    count_rhs = values.shape[0]
    width = values.shape[1] // 4
    groups = table.shape[1]
    parts = values.reshape(count_rhs, 4, groups, -1)
    back_left = jnp.einsum("jk,rjb->rkb", table[0], parts[:, 0], precision=HIGH).reshape(
        count_rhs, width
    )
    back_low = jnp.einsum("jk,rjb->rkb", table[1], parts[:, 2], precision=HIGH).reshape(
        count_rhs, width
    )
    from_right = passed_along(back_left, "gx", -1)
    from_above = passed_along(back_low, "gy", -1)
    out = jnp.stack(
        [values[:, width : 2 * width] - from_right, values[:, 3 * width :] - from_above], axis=0
    )
    return out * live


def inner_local(first, second):
    return jnp.sum(first * second, axis=(0, 2))


def precond_dot(first, second):
    return lax.psum(inner_local(first, second), ("gx", "gy"))


def on_device(load, schur_inv, schur, coupling, pairing, corner_rows, coarse_inv):
    field0 = load[0, 0]
    count_rhs = field0.shape[1]
    inverse = schur_inv[0, 0]
    stiffness = schur[0, 0]
    couple = coupling[0, 0]
    rows = corner_rows[0, 0]
    groups = pairing.shape[-1]
    table = (
        pairing[0, 0][:, :, None] == jnp.arange(groups, dtype=jnp.int32)[None, None, :]
    ).astype(jnp.float32)
    table_half = table.astype(jnp.bfloat16)
    right_live = (lax.axis_index("gx") < lax.axis_size("gx") - 1).astype(jnp.float32)
    upper_live = (lax.axis_index("gy") < lax.axis_size("gy") - 1).astype(jnp.float32)
    live = jnp.stack([right_live, upper_live])[:, None, None]
    block_rows = coarse_inv.shape[1]
    device_count = lax.axis_size("gx") * lax.axis_size("gy")
    order = block_rows * device_count

    def precond(field):
        assembled = assemble((0.5 * field).astype(jnp.bfloat16), table_half)
        return 0.5 * jump(
            jnp.dot(assembled, stiffness, preferred_element_type=jnp.float32), table, live
        )

    residual = field0 * live
    multipliers = jnp.zeros_like(residual)
    search = precond(residual)
    direction = search
    norm_now = precond_dot(residual, search)
    for step in range(ITERS):
        operator_assembled = assemble(direction.astype(jnp.bfloat16), table_half)
        values = jnp.dot(operator_assembled, inverse, preferred_element_type=jnp.float32)
        operator_corner = jnp.dot(
            values.astype(jnp.bfloat16), couple, preferred_element_type=jnp.float32
        )
        partial_sum = jnp.zeros((count_rhs, order), jnp.float32).at[:, rows].add(operator_corner)
        mine = lax.psum_scatter(partial_sum, ("gx", "gy"), scatter_dimension=1, tiled=True)
        solved = jnp.dot(mine, coarse_inv, precision=HIGH).astype(jnp.bfloat16)
        picked = lax.all_gather(solved, ("gx", "gy"), axis=1, tiled=True)[:, rows]
        lifted = jnp.dot(picked, couple.T, preferred_element_type=jnp.float32).astype(jnp.bfloat16)
        full_values = values + jnp.dot(lifted, inverse, preferred_element_type=jnp.float32)
        image = jump(full_values, table, live)
        alpha = norm_now / lax.psum(inner_local(direction, image), ("gx", "gy"))
        multipliers = multipliers + alpha[:, None] * direction
        residual = residual - alpha[:, None] * image
        if step + 1 < ITERS:
            search = precond(residual)
            norm_next = precond_dot(residual, search)
            direction = search + (norm_next / norm_now)[:, None] * direction
            norm_now = norm_next
    return (multipliers[None, None], residual[None, None])


def solution(mesh):
    placed = (
        P("gx", "gy", None, None, None),
        P("gx", "gy", None, None),
        P("gx", "gy", None, None),
        P("gx", "gy", None, None),
        P("gx", "gy", None, None),
        P("gx", "gy", None),
        P(("gx", "gy"), None),
    )
    return jax.shard_map(
        on_device,
        mesh=mesh,
        in_specs=placed,
        out_specs=(P("gx", "gy", None, None, None), P("gx", "gy", None, None, None)),
        check_vma=False,
    )
```

profile of v0, /device:TPU:1, one launch (start us, length us, event | category | flops | bytes accessed | tf_op | source)
XLA Modules:
  0.0 1416.1 jit_solution(5267901932098409480)
XLA Ops:
  8.5 4.6 collective-permute-start
  19.0 4.7 fusion.16
  37.2 4.7 collective-permute-start.4
  47.5 4.6 fusion.10
  56.8 215.8 %reduce-scatter.4.cloned.1.call-done = f32[112,96]{0,1:T(8,128)} async-done(((f32[112,12288]{0,1:T(8,128)}), f32[112,96]{0,1:T(8,128)}) %reduce-scatter.4.cloned.1.call-update) | async-done | bytes 43024 | tf_op jit(solution)/shard_map/reduce_scatter | solution.py:104
  274.3 67.8 %all-gather.4.cloned.1.call-done = bf16[112,12288]{0,1:T(8,128)(2,1)} async-done(((bf16[112,96]{0,1:T(8,128)(2,1)}), bf16[112,12288]{0,1:T(8,128)(2,1)}) %all-gather.4.cloned.1.call-update) | async-done | bytes 2752528 | tf_op jit(solution)/shard_map/all_gather | solution.py:106
  345.7 5.0 fusion.24
  364.7 64.6 %all-reduce = (f32[112]{0:T(128)S(1)}, f32[112]{0:T(128)S(1)}) all-reduce(f32[112]{0:T(128)S(1)} %get-tuple-element.3, f32[112]{0:T(128)S(1)} %get-tuple-element.2), channel_id=1, replica_groups=mesh['gx'=8,'gy'=16] {'gx','gy'}, use_global_device_ids=true, to_apply=%region_1.0 | all-reduce | flops 224 | bytes 1792 | tf_op jit(solution)/shard_map/psum | solution.py:64
  438.9 4.7 fusion.14
  451.1 4.4 collective-permute-done.10
  461.2 67.1 %psum.44 = f32[112]{0:T(128)S(1)} all-reduce(f32[112]{0:T(128)S(1)} %multiply_reduce_fusion.2), channel_id=1, replica_groups=mesh['gx'=8,'gy'=16] {'gx','gy'}, use_global_device_ids=true, to_apply=%region_7.0 | all-reduce | flops 112 | bytes 896 | tf_op jit(solution)/shard_map/psum | solution.py:64
  538.4 4.8 fusion.6
  547.8 211.2 %reduce-scatter.6.cloned.1.call-done = f32[112,96]{0,1:T(8,128)} async-done(((f32[112,12288]{0,1:T(8,128)}), f32[112,96]{0,1:T(8,128)}) %reduce-scatter.6.cloned.1.call-update) | async-done | bytes 43024 | tf_op jit(solution)/shard_map/reduce_scatter | solution.py:104
  761.0 67.1 %all-gather.6.cloned.1.call-done = bf16[112,12288]{0,1:T(8,128)(2,1)} async-done(((bf16[112,96]{0,1:T(8,128)(2,1)}), bf16[112,12288]{0,1:T(8,128)(2,1)}) %all-gather.6.cloned.1.call-update) | async-done | bytes 2752528 | tf_op jit(solution)/shard_map/all_gather | solution.py:106
  831.1 5.9 fusion.27
  853.1 64.5 %psum.45 = f32[112]{0:T(128)S(1)} all-reduce(f32[112]{0:T(128)S(1)} %multiply_reduce_fusion.1), channel_id=1, replica_groups=mesh['gx'=8,'gy'=16] {'gx','gy'}, use_global_device_ids=true, to_apply=%region_11.0 | all-reduce | flops 112 | bytes 896 | tf_op jit(solution)/shard_map/psum | solution.py:110
  926.5 5.0 fusion.12
  939.0 4.4 collective-permute-done.18
  949.0 67.4 %psum.46 = f32[112]{0:T(128)S(1)} all-reduce(f32[112]{0:T(128)S(1)} %multiply_reduce_fusion), channel_id=1, replica_groups=mesh['gx'=8,'gy'=16] {'gx','gy'}, use_global_device_ids=true, to_apply=%region_13.0 | all-reduce | flops 112 | bytes 896 | tf_op jit(solution)/shard_map/psum | solution.py:64
  1026.5 4.8 fusion.2
  1036.0 211.2 %reduce-scatter.8.cloned.1.call-done = f32[112,96]{0,1:T(8,128)} async-done(((f32[112,12288]{0,1:T(8,128)}), f32[112,96]{0,1:T(8,128)}) %reduce-scatter.8.cloned.1.call-update) | async-done | bytes 43024 | tf_op jit(solution)/shard_map/reduce_scatter | solution.py:104
  1248.9 67.2 %all-gather.8.cloned.1.call-done = bf16[112,12288]{0,1:T(8,128)(2,1)} async-done(((bf16[112,96]{0,1:T(8,128)(2,1)}), bf16[112,12288]{0,1:T(8,128)(2,1)}) %all-gather.8.cloned.1.call-update) | async-done | bytes 2752528 | tf_op jit(solution)/shard_map/all_gather | solution.py:106
  1319.7 4.9 fusion.30
  1338.9 64.5 %psum.47 = f32[112]{0:T(128)S(1)} all-reduce(f32[112]{0:T(128)S(1)} %fusion.101), channel_id=1, replica_groups=mesh['gx'=8,'gy'=16] {'gx','gy'}, use_global_device_ids=true, to_apply=%region_17.0 | all-reduce | flops 112 | bytes 896 | tf_op jit(solution)/shard_map/psum | solution.py:110
  (211 shorter events, 169.9 us)
Async XLA Ops:
  7.2 265.4 %reduce-scatter.4.cloned.1.call-start = ((), (), s32[]{:S(2)}) async-start(), calls=%async_computation.3 | async-start | bytes 6340608 | tf_op jit(solution)/shard_map/reduce_scatter | solution.py:104
  8.5 8.9 collective-permute-start
  13.1 5.6 collective-permute-start.1
  25.2 7.6 collective-permute-start.2
  27.1 9.0 collective-permute-start.3
  37.2 8.3 collective-permute-start.4
  56.7 285.4 %all-gather.4.cloned.1.call-start = ((), (), s32[]{:S(2)}) async-start(), calls=%async_computation.4 | async-start | bytes 3170304 | tf_op jit(solution)/shard_map/all_gather | solution.py:106
  274.2 484.8 %reduce-scatter.6.cloned.1.call-start = ((), (), s32[]{:S(2)}) async-start(), calls=%async_computation.5 | async-start | bytes 6340608 | tf_op jit(solution)/shard_map/reduce_scatter | solution.py:104
  352.2 7.6 collective-permute-start.6
  354.4 9.2 collective-permute-start.7
  432.6 5.3 collective-permute-start.9
  447.9 7.6 collective-permute-start.10
  449.8 9.6 collective-permute-start.11
  547.8 280.3 %all-gather.6.cloned.1.call-start = ((), (), s32[]{:S(2)}) async-start(), calls=%async_computation.6 | async-start | bytes 3170304 | tf_op jit(solution)/shard_map/all_gather | solution.py:106
  760.8 486.5 %reduce-scatter.8.cloned.1.call-start = ((), (), s32[]{:S(2)}) async-start(), calls=%async_computation.7 | async-start | bytes 6340608 | tf_op jit(solution)/shard_map/reduce_scatter | solution.py:104
  839.6 7.6 collective-permute-start.14
  841.7 9.2 collective-permute-start.15
  918.4 5.4 collective-permute-start.16
  920.9 5.3 collective-permute-start.17
  935.7 7.6 collective-permute-start.18
  937.7 9.5 collective-permute-start.19
  1036.0 280.1 %all-gather.8.cloned.1.call-start = ((), (), s32[]{:S(2)}) async-start(), calls=%async_computation.8 | async-start | bytes 3170304 | tf_op jit(solution)/shard_map/all_gather | solution.py:106
  1326.1 7.6 collective-permute-start.22
  1328.3 9.2 collective-permute-start.23
  (28 other events, 1835.4 us)
Sparse Core Ops, SparseCore 0:
  56.9 215.6 reduce-scatter.3
  276.7 65.4 all-gather.3
  547.9 211.0 reduce-scatter.5
  762.6 65.4 all-gather.5
  1036.1 211.0 reduce-scatter.7
  1250.6 65.4 all-gather.7
where the time goes:
time: 1430 us; the launch traced here: 1420 us
  waiting for transfers between devices  897 us (63%)
  blocking collectives  328 us (23%)
  matrix products  65.1 us (5%)
  starting transfers between devices  56.8 us (4%)
  other arithmetic  32.6 us (2%)
  local copies, waits for them, and re-layouts  20.7 us (1%)
  between operations  15.6 us (1%)
    reduce_scatter x3, waiting for transfers between devices, on_device(): lax.psum_scatter(partial_sum, ('gx', 'gy'), scatter_dimension=1, tiled=True)  638 us
    all_gather x3, waiting for transfers between devices, on_device(): picked = lax.all_gather(solved, ('gx', 'gy'), axis=1, tiled=True)[:, rows]  202 us
    psum x3, blocking collectives, precond_dot(): return lax.psum(inner_local(first, second), ('gx', 'gy'))  199 us
    psum x2, blocking collectives, on_device(): alpha = norm_now / lax.psum(inner_local(direction, image), ('gx', 'gy'))  129 us
    ppermute x24, waiting for transfers between devices, passed_along(): lax.ppermute(value, axis, [(source, source + steps) for source in range(f...  56.8 us
    ppermute x24, starting transfers between devices, passed_along(): lax.ppermute(value, axis, [(source, source + steps) for source in range(f...  56.4 us
  transfers between devices with their start and end apart: 30, of which 24 were waited for; matrix products, arithmetic and copies ran while one was open for 0% of the time, Pallas kernels for 0%

commit v1 on v0

v1 whole, which is shorter than its diff:
```python
import functools

import jax
import jax.numpy as jnp
from jax import lax
from jax.experimental import pallas as pl
from jax.experimental.pallas import tpu as pltpu
from jax.sharding import PartitionSpec as P

ITERS = 3
MESH = pl.DeviceIdType.MESH
BF = jnp.bfloat16
F32 = jnp.float32
LANES = 128
WIDTH = 4


def log2(value):
    return value.bit_length() - 1


def radices(nx, ny):
    return (nx // 2, 2, max(1, ny // 4), min(4, ny))


def offsets_far_first(rad):
    dy, dc, dx, dz = rad
    found = [
        (y, c, x, z) for y in range(dy) for c in range(dc) for x in range(dx) for z in range(dz)
    ]

    def hops(t):
        chips = sum(min(d, r - d) for d, r in ((t[0], dy), (t[2], dx), (t[3], dz)))
        return 2 * chips + t[1]

    return sorted(found[1:], key=hops, reverse=True)


def kernel(
    nx, ny,
    load_ref, inverse_hbm, stiff_hbm, couple_hbm, pair_ref, row_ref, col_ref, coarse_ref,
    mult_ref, res_ref,
    inverse, stiff, couple, lift, drop, solve, coarse_pad,
    resid, direc, image, prec, fresh, mult, weights, values,
    slots, sent0, got0, sent1, got1, sent2, got2, owned, square, *rest,
):
    halo_send = (rest[0:4], rest[4:8])
    halo_got = (rest[8:12], rest[12:16])
    load_sem, halo_ssem, halo_rsem, all_ssem, all_rsem = rest[16:21]
    rhs = load_ref.shape[1]
    face = load_ref.shape[2]
    groups = face // LANES
    corners = row_ref.shape[1]
    count = nx * ny
    rad = radices(nx, ny)
    order = offsets_far_first(rad)
    a, b = lax.axis_index("gx"), lax.axis_index("gy")
    my_y, my_c, my_x, my_z = a // 2, lax.rem(a, 2), b // rad[3], lax.rem(b, rad[3])

    def device(t, sign):
        y, c, x, z = (
            lax.rem(mine + sign * step + radix, radix)
            for mine, step, radix in zip((my_y, my_c, my_x, my_z), t, rad)
        )
        return (y * 2 + c, x * rad[3] + z)

    def place(t):
        return ((t[0] * rad[1] + t[1]) * rad[2] + t[2]) * rad[3] + t[3]

    copies = [
        pltpu.make_async_copy(source, target, load_sem.at[i])
        for i, (source, target) in enumerate(
            ((couple_hbm, couple), (inverse_hbm, inverse), (stiff_hbm, stiff))
        )
    ]
    for copy in copies:
        copy.start()

    barrier = pltpu.get_barrier_semaphore()
    for t in order:
        pl.semaphore_signal(barrier, inc=1, device_id=device(t, 1), device_id_type=MESH)

    right_live = (a < nx - 1).astype(F32)
    left_live = (a > 0).astype(F32)
    upper_live = (b < ny - 1).astype(F32)
    lower_live = (b > 0).astype(F32)
    neighbours = (
        (lax.rem(a + 1, nx), b),
        (lax.rem(a + nx - 1, nx), b),
        (a, lax.rem(b + 1, ny)),
        (a, lax.rem(b + ny - 1, ny)),
    )

    def halo_copy(which, way):
        return pltpu.make_async_remote_copy(
            src_ref=halo_send[which][way],
            dst_ref=halo_got[which][way],
            send_sem=halo_ssem.at[which, way],
            recv_sem=halo_rsem.at[which, way],
            device_id=neighbours[way],
            device_id_type=MESH,
        )

    def all_start(which, source, target, sign):
        for t in order:
            rows = pl.ds(place(t) * WIDTH, WIDTH)
            pltpu.make_async_remote_copy(
                src_ref=source.at[rows],
                dst_ref=target.at[rows],
                send_sem=all_ssem.at[which],
                recv_sem=all_rsem.at[which],
                device_id=device(t, sign),
                device_id_type=MESH,
            ).start()
        target[0:WIDTH] = source[0:WIDTH]

    def all_wait(which, source, target):
        rows = pl.ds(WIDTH, (count - 1) * WIDTH)
        pltpu.make_async_remote_copy(
            src_ref=source.at[rows],
            dst_ref=target.at[rows],
            send_sem=all_ssem.at[which],
            recv_sem=all_rsem.at[which],
            device_id=neighbours[0],
            device_id_type=MESH,
        ).wait()

    def slot_of(rows):
        block = (rows * 43691) >> 22
        z = block & (rad[3] - 1)
        x = (block >> log2(rad[3])) & (rad[2] - 1)
        gx = block >> log2(rad[2] * rad[3])
        c = gx & 1
        y = gx >> 1
        dy = (y - my_y + rad[0]) & (rad[0] - 1)
        dc = (c - my_c + 2) & 1
        dx = (x - my_x + rad[2]) & (rad[2] - 1)
        dz = (z - my_z + rad[3]) & (rad[3] - 1)
        return block, rows - block * 96, place((dy, dc, dx, dz)) * WIDTH

    block_row, offset_row, slot_row = slot_of(row_ref[...])
    block_col, offset_col, slot_col = slot_of(col_ref[...])
    at_col = lax.broadcasted_iota(jnp.int32, (corners, corners), 0)
    at_row = lax.broadcasted_iota(jnp.int32, (corners, corners), 1)
    same = block_row == block_col
    rank_col = jnp.sum((same & (at_row < at_col)).astype(F32), axis=1, keepdims=True)
    rank_row = jnp.sum((same & (at_col < at_row)).astype(F32), axis=0, keepdims=True)
    slot_col = slot_col + rank_col.astype(jnp.int32)
    slot_row = slot_row + rank_row.astype(jnp.int32)
    total = count * WIDTH
    hot = (slot_col == lax.broadcasted_iota(jnp.int32, (corners, total), 1)).astype(F32).astype(BF)
    hot_t = slot_row == lax.broadcasted_iota(jnp.int32, (total, corners), 0)
    offset = jnp.sum(
        jnp.where(hot_t, offset_row.astype(F32) - 200.0, 0.0), axis=1, keepdims=True
    )
    sent0[...] = jnp.broadcast_to(offset + 200.0, (total, LANES))

    coarse_pad[...] = jnp.zeros_like(coarse_pad)
    coarse_pad[0 : coarse_ref.shape[0], 0 : coarse_ref.shape[1]] = coarse_ref[...]
    slots[...] = jnp.zeros_like(slots)
    square[...] = jnp.zeros_like(square)
    for ref in (direc, image, mult, owned):
        ref[...] = jnp.zeros_like(ref)
    for k in range(groups):
        part = slice(k * LANES, (k + 1) * LANES)
        halo_send[0][0][k] = load_ref[0, :, part].astype(BF)
        halo_send[0][2][k] = load_ref[1, :, part].astype(BF)

    pl.semaphore_wait(barrier, count - 1)
    first = [halo_copy(0, 2), halo_copy(0, 0)]
    for copy in first:
        copy.start()
    all_start(0, sent0, got0, 1)

    copies[0].wait()
    copies[1].wait()
    product = jnp.dot(inverse[...], couple[...], preferred_element_type=F32).astype(BF)
    spread = jnp.dot(product, hot, preferred_element_type=F32)
    drop[...] = spread.astype(BF)
    for k in range(4 * groups):
        part = slice(k * LANES, (k + 1) * LANES)
        lift[:, part] = spread[part].T.astype(BF)

    def block(f, k):
        return slice((f * groups + k) * LANES, (f * groups + k + 1) * LANES)

    def put_resid(f, k, value):
        resid[:, block(f, k)] = value
        weights[:, block(f, k)] = (0.5 * value).astype(BF)

    for copy in first:
        copy.wait()
    for k in range(groups):
        part = slice(k * LANES, (k + 1) * LANES)
        put_resid(1, k, load_ref[0, :, part] * right_live)
        put_resid(3, k, load_ref[1, :, part] * upper_live)
        put_resid(0, k, -halo_got[0][0][pair_ref[0, k]].astype(F32) * left_live)
        put_resid(2, k, -halo_got[0][2][pair_ref[1, k]].astype(F32) * lower_live)

    all_wait(0, sent0, got0)
    lane = lax.broadcasted_iota(jnp.int32, (total, LANES), 1).astype(F32)
    pick = (got0[...] == lane).astype(F32).astype(BF)
    wide = jnp.dot(pick, coarse_pad[...].astype(BF), preferred_element_type=F32).astype(BF)
    solve[...] = lax.dot_general(
        wide, pick, (((1,), (1,)), ((), ())), preferred_element_type=F32
    ).astype(BF)
    copies[2].wait()

    inverse_pair = [
        [
            sum(j * (pair_ref[side, j] == k).astype(jnp.int32) for j in range(groups))
            for k in range(groups)
        ]
        for side in range(2)
    ]

    def send_faces(which, side):
        low, high = (0, 1) if side == 0 else (2, 3)
        for k in range(groups):
            halo_send[which][high - 1][k] = values[high * groups + k].astype(BF)
            halo_send[which][high][k] = values[low * groups + inverse_pair[side][k]].astype(BF)
        sent = [halo_copy(which, high - 1), halo_copy(which, high)]
        for copy in sent:
            copy.start()
        return sent

    def jumped(which, f, k):
        own = values[f * groups + k]
        if f == 0:
            return (own - halo_got[which][0][pair_ref[0, k]].astype(F32)) * left_live
        if f == 1:
            return (own - halo_got[which][1][k].astype(F32)) * right_live
        if f == 2:
            return (own - halo_got[which][2][pair_ref[1, k]].astype(F32)) * lower_live
        return (own - halo_got[which][3][k].astype(F32)) * upper_live

    lane_slot = lax.broadcasted_iota(jnp.int32, (rhs, total), 1) & (WIDTH - 1)
    row_slot = lax.broadcasted_iota(jnp.int32, (total, LANES), 0) & (WIDTH - 1)
    real = lax.broadcasted_iota(jnp.int32, (1, LANES), 1) < rhs

    def as_row(value):
        square[0:rhs, :] = value
        return jnp.sum(square[...].T, axis=0, keepdims=True)

    def as_columns(row):
        return jnp.broadcast_to(row, (LANES, LANES)).T[0:rhs]

    def dots_row(received):
        return jnp.sum(jnp.where(row_slot == WIDTH - 1, received, 0.0), axis=0, keepdims=True)

    def iteration(step, carry):
        norm_before, local_before = carry
        later = (step > 0).astype(F32)

        sent = []
        norm_part = jnp.zeros((rhs, LANES), F32)
        for side in (1, 0):
            for f in ((2, 3), (0, 1))[1 - side]:
                out = jnp.dot(
                    weights[...], stiff[:, f * face : (f + 1) * face], preferred_element_type=F32
                )
                for k in range(groups):
                    values[f * groups + k] = out[:, k * LANES : (k + 1) * LANES]
            sent += send_faces(1, side)
        for f in range(4):
            for k in range(groups):
                norm_part = norm_part + resid[:, block(f, k)] * values[f * groups + k]
        norm_col = 0.5 * jnp.sum(norm_part, axis=1, keepdims=True)
        for copy in sent:
            copy.wait()
        for f in range(4):
            for k in range(groups):
                z = 0.5 * jumped(1, f, k)
                prec[:, block(f, k)] = z
                weights[:, block(f, k)] = z.astype(BF)

        spread_out = jnp.dot(weights[...], drop[...], preferred_element_type=F32)
        slots[0:rhs, :] = jnp.where(lane_slot == WIDTH - 1, norm_col, spread_out)
        sent1[...] = slots[...].T
        all_start(1, sent1, got1, 1)

        part_new = jnp.zeros((rhs, LANES), F32)
        part_mix = jnp.zeros((rhs, LANES), F32)
        for f in range(4):
            out = jnp.dot(
                weights[...], inverse[:, f * face : (f + 1) * face], preferred_element_type=F32
            )
            for k in range(groups):
                at = block(f, k)
                v = out[:, k * LANES : (k + 1) * LANES]
                fresh[:, at] = v
                part_new = part_new + prec[:, at] * v
                part_mix = part_mix + (prec[:, at] * image[:, at] + direc[:, at] * v)
        dot_new = as_row(part_new)
        dot_mix = as_row(part_mix)

        all_wait(1, sent1, got1)
        received = got1[...]
        norm = dots_row(received)
        beta = jnp.where(real, norm / norm_before, 0.0) * later
        owned[...] = received + beta * owned[...]
        sums = owned[...]
        solved = jnp.dot(solve[...], sums.astype(BF), preferred_element_type=F32)
        local = dot_new + beta * (dot_mix + beta * local_before)
        energy = local + jnp.sum(sums * solved, axis=0, keepdims=True)
        sent2[...] = jnp.where(row_slot == WIDTH - 1, energy, solved)
        all_start(2, sent2, got2, -1)

        beta_cols = as_columns(beta)
        for k in range(4 * groups):
            at = slice(k * LANES, (k + 1) * LANES)
            direc[:, at] = prec[:, at] + beta_cols * direc[:, at]
            image[:, at] = fresh[:, at] + beta_cols * image[:, at]

        all_wait(2, sent2, got2)
        received = got2[...]
        alpha = jnp.where(real, norm / dots_row(received), 0.0)
        picked = received.T[0:rhs].astype(BF)
        sent = []
        for side in (1, 0):
            for f in ((2, 3), (0, 1))[1 - side]:
                at = slice(f * face, (f + 1) * face)
                out = image[:, at] + jnp.dot(picked, lift[:, at], preferred_element_type=F32)
                for k in range(groups):
                    values[f * groups + k] = out[:, k * LANES : (k + 1) * LANES]
            sent += send_faces(0, side)
        alpha_cols = as_columns(alpha)
        for k in range(groups):
            for i, f in enumerate((1, 3)):
                part = slice((i * groups + k) * LANES, (i * groups + k + 1) * LANES)
                mult[:, part] = mult[:, part] + alpha_cols * direc[:, block(f, k)]
        for copy in sent:
            copy.wait()
        for f in range(4):
            for k in range(groups):
                put_resid(f, k, resid[:, block(f, k)] - alpha_cols * jumped(0, f, k))
        return norm, local

    start = (jnp.ones((1, LANES), F32), jnp.zeros((1, LANES), F32))
    lax.fori_loop(0, ITERS, iteration, start)
    for i, f in enumerate((1, 3)):
        mult_ref[i] = mult[:, i * face : (i + 1) * face]
        res_ref[i] = resid[:, f * face : (f + 1) * face]


def on_device(nx, ny, load, schur_inv, schur, coupling, pairing, corner_rows, coarse_inv):
    field = load[0, 0]
    rhs, face = field.shape[1:]
    width = 4 * face
    groups = face // LANES
    corners = corner_rows.shape[-1]
    total = nx * ny * WIDTH
    vmem = pl.BlockSpec(memory_space=pltpu.VMEM)
    hbm = pl.BlockSpec(memory_space=pl.ANY)
    smem = pl.BlockSpec(memory_space=pltpu.SMEM)
    halo = pltpu.VMEM((groups, rhs, LANES), BF)
    chunk = pltpu.VMEM((total, LANES), F32)
    state = pltpu.VMEM((rhs, width), F32)
    dma = pltpu.SemaphoreType.DMA
    out = jax.ShapeDtypeStruct(field.shape, F32)
    mult, res = pl.pallas_call(
        functools.partial(kernel, nx, ny),
        out_shape=(out, out),
        in_specs=[vmem, hbm, hbm, hbm, smem, vmem, vmem, vmem],
        out_specs=(vmem, vmem),
        scratch_shapes=[
            pltpu.VMEM((width, width), BF),
            pltpu.VMEM((width, width), BF),
            pltpu.VMEM((width, corners), BF),
            pltpu.VMEM((total, width), BF),
            pltpu.VMEM((width, total), BF),
            pltpu.VMEM((total, total), BF),
            pltpu.VMEM((LANES, LANES), F32),
            state, state, state, state, state,
            pltpu.VMEM((rhs, 2 * face), F32),
            pltpu.VMEM((rhs, width), BF),
            pltpu.VMEM((4 * groups, rhs, LANES), F32),
            pltpu.VMEM((LANES, total), F32),
            chunk, chunk, chunk, chunk, chunk, chunk, chunk,
            pltpu.VMEM((LANES, LANES), F32),
            *([halo] * 16),
            dma((3,)), dma((2, 4)), dma((2, 4)), dma((3,)), dma((3,)),
        ],
        compiler_params=pltpu.CompilerParams(
            collective_id=0, has_side_effects=True, vmem_limit_bytes=58 * 2**20
        ),
        name="feti",
    )(
        field, schur_inv[0, 0], schur[0, 0], coupling[0, 0], pairing[0, 0],
        corner_rows[0], corner_rows[0, 0][:, None], coarse_inv,
    )
    return (mult[None, None], res[None, None])


def solution(mesh):
    placed = (
        P("gx", "gy", None, None, None),
        P("gx", "gy", None, None),
        P("gx", "gy", None, None),
        P("gx", "gy", None, None),
        P("gx", "gy", None, None),
        P("gx", "gy", None),
        P(("gx", "gy"), None),
    )
    return jax.shard_map(
        functools.partial(on_device, mesh.shape["gx"], mesh.shape["gy"]),
        mesh=mesh,
        in_specs=placed,
        out_specs=(P("gx", "gy", None, None, None), P("gx", "gy", None, None, None)),
        check_vma=False,
    )
```

time: 1430 us -> 109 us (0.08)
  waiting for transfers between devices: 897 us -> 0 us
  blocking collectives: 328 us -> 0 us
  Pallas kernels: 0 us -> 101 us
  matrix products: 65.1 us -> 0 us
  starting transfers between devices: 56.8 us -> 0 us
  other arithmetic: 32.6 us -> 0 us
  between operations: 15.6 us -> 0.64 us
    reduce_scatter x3 -> x0, waiting for transfers between devices: 638 us -> none  [on_device(): lax.psum_scatter(partial_sum, ('gx', 'gy'), scatter_dimension=1, tiled=True)]
    psum x5 -> x0, blocking collectives: 328 us -> none  [the longest x3 199 us: precond_dot(): return lax.psum(inner_local(first, second), ('gx', 'gy'))]
    all_gather x3 -> x0, waiting for transfers between devices: 202 us -> none  [on_device(): picked = lax.all_gather(solved, ('gx', 'gy'), axis=1, tiled=True)[:, rows]]
    pallas_call x0 -> x1, Pallas kernels: none -> 101 us  [on_device(): pl.pallas_call(functools.partial(kernel, nx, ny), out_shape=(out, out), i...]
    dot_general x39 -> x0, matrix products: 65.1 us -> none  [the longest x3 15.8 us: on_device(): jnp.dot(lifted, inverse, preferred_element_type=jnp.float32)]
    ppermute x24 -> x0, waiting for transfers between devices: 56.8 us -> none  [passed_along(): lax.ppermute(value, axis, [(source, source + steps) for source in range(f...]
    ppermute x24 -> x0, starting transfers between devices: 56.4 us -> none  [passed_along(): lax.ppermute(value, axis, [(source, source + steps) for source in range(f...]
  transfers between devices with their start and end apart: 30 -> 0, of which waited for: 24 -> 0; matrix products, arithmetic and copies ran while one was open for 0% -> 0% of each run, Pallas kernels for 0% -> 0%
where the time goes in v1:
time: 109 us
  Pallas kernels  101 us (93%)
  local copies, waits for them, and re-layouts  7.31 us (7%)
    pallas_call x1, Pallas kernels, on_device(): pl.pallas_call(functools.partial(kernel, nx, ny), out_shape=(out, out), i...  101 us
    unnamed x3, local copies, waits for them, and re-layouts  5.86 us

profile of v1, /device:TPU:1, one launch (start us, length us, event | category | flops | bytes accessed | tf_op | source)
XLA Modules:
  0.0 109.1 jit_solution(12163727945384617569)
XLA Ops:
  0.6 1.4 %copy.11.col_ref = s32[192,1]{1,0:T(8,128)} copy(s32[192,1]{0,1:T(1,128)} %bitcast.15) | data formatting | bytes 1536 | tf_op jit(solution)/shard_map/broadcast_in_dim;squeeze | solution.py:390
  2.1 2.2 %copy.10 = bf16[1,1,2048,192]{3,2,1,0:T(8,128)(2,1)} copy(bf16[1,1,2048,192]{2,3,1,0:T(8,128)(2,1)} %param.10) | data formatting | bytes 1572864 | tf_op args[3]
  4.3 101.2 %feti.1 = (f32[2,112,512]{2,1,0:T(8,128)}, f32[2,112,512]{2,1,0:T(8,128)}) custom-call(f32[2,112,512]{2,1,0:T(8,128)} %bitcast.14, bf16[2048,2048]{1,0:T(8,128)(2,1)} %bitcast.9, bf16[2048,2048]{1,0:T(8,128)(2,1)} %bitcast.10, bf16[2048,192]{1,0:T(8,128)(2,1)} %bitcast.11, s32[2,4]{1,0:T(2,128)} %bitcast.17, s32[1,192]{1,0:T(1,128)} %bitcast.16, ...), custom_call_target="tpu_custom_call" | custom-call | tf_op jit(solution)/shard_map/feti/pallas_call | solution.py:361
  105.5 1.8 %copy.14 = f32[1,1,2,112,512]{4,3,2,1,0:T(8,128)} copy(f32[1,1,2,112,512]{4,3,2,1,0:T(8,128)} %bitcast.13) | data formatting | bytes 917504
  107.3 1.8 %copy.15 = f32[1,1,2,112,512]{4,3,2,1,0:T(8,128)} copy(f32[1,1,2,112,512]{4,3,2,1,0:T(8,128)} %bitcast.12) | data formatting | bytes 917504

commit v2 on v1

v2 whole, which is shorter than its diff:
```python
import functools

import jax
import jax.numpy as jnp
from jax import lax
from jax.experimental import pallas as pl
from jax.experimental.pallas import tpu as pltpu
from jax.sharding import PartitionSpec as P

ITERS = 3
MESH = pl.DeviceIdType.MESH
BF = jnp.bfloat16
F32 = jnp.float32
LANES = 128
WIDTH = 4


def log2(value):
    return value.bit_length() - 1


def radices(nx, ny):
    return (nx // 2, 2, max(1, ny // 4), min(4, ny))


def offsets_far_first(rad):
    dy, dc, dx, dz = rad
    found = [
        (y, c, x, z) for y in range(dy) for c in range(dc) for x in range(dx) for z in range(dz)
    ]

    def hops(t):
        chips = sum(min(d, r - d) for d, r in ((t[0], dy), (t[2], dx), (t[3], dz)))
        return 2 * chips + t[1]

    return sorted(found[1:], key=hops, reverse=True)


def kernel(
    nx, ny,
    load_ref, inverse_hbm, stiff_hbm, couple_hbm, pair_ref, row_ref, coarse_ref,
    mult_ref, res_ref,
    inverse, stiff, couple, drop, solve, gather, coarse_pad,
    resid, direc, image, wave, whole, prec, mult, weights, values, norm_part,
    wide_row, slots, sent0, got0, sent1, got1, sent2, got2, owned, square, corner_mine, face_low, *rest,
):
    halo_send = (rest[0:4], rest[4:8])
    halo_got = (rest[8:12], rest[12:16])
    face_send, face_got = rest[16:20], rest[20:24]
    lift, corner_got = rest[24:28], rest[28:32]
    load_sem, halo_ssem, halo_rsem, all_ssem, all_rsem = rest[32:37]
    face_ssem, face_rsem, corner_ssem, corner_rsem = rest[37:41]
    rhs = load_ref.shape[1]
    face = load_ref.shape[2]
    groups = face // LANES
    corners = row_ref.shape[1]
    held = corner_mine.shape[1]
    count = nx * ny
    total = count * WIDTH
    rad = radices(nx, ny)
    order = offsets_far_first(rad)
    a, b = lax.axis_index("gx"), lax.axis_index("gy")
    my_y, my_c, my_x, my_z = a // 2, lax.rem(a, 2), b // rad[3], lax.rem(b, rad[3])

    def device(t, sign):
        y, c, x, z = (
            lax.rem(mine + sign * step + radix, radix)
            for mine, step, radix in zip((my_y, my_c, my_x, my_z), t, rad)
        )
        return (y * 2 + c, x * rad[3] + z)

    def place(t):
        return ((t[0] * rad[1] + t[1]) * rad[2] + t[2]) * rad[3] + t[3]

    copies = [
        pltpu.make_async_copy(source, target, load_sem.at[i])
        for i, (source, target) in enumerate(
            ((couple_hbm, couple), (inverse_hbm, inverse), (stiff_hbm, stiff))
        )
    ]
    for copy in copies:
        copy.start()

    barrier = pltpu.get_barrier_semaphore()
    for t in order:
        pl.semaphore_signal(barrier, inc=1, device_id=device(t, 1), device_id_type=MESH)

    live = (
        (a > 0).astype(F32),
        (a < nx - 1).astype(F32),
        (b > 0).astype(F32),
        (b < ny - 1).astype(F32),
    )
    neighbours = (
        (lax.rem(a + 1, nx), b),
        (lax.rem(a + nx - 1, nx), b),
        (a, lax.rem(b + 1, ny)),
        (a, lax.rem(b + ny - 1, ny)),
    )

    def halo_copy(which, way):
        return pltpu.make_async_remote_copy(
            src_ref=halo_send[which][way],
            dst_ref=halo_got[which][way],
            send_sem=halo_ssem.at[which, way],
            recv_sem=halo_rsem.at[which, way],
            device_id=neighbours[way],
            device_id_type=MESH,
        )

    def face_copy(way):
        return pltpu.make_async_remote_copy(
            src_ref=face_send[way],
            dst_ref=face_got[way],
            send_sem=face_ssem.at[way],
            recv_sem=face_rsem.at[way],
            device_id=neighbours[way],
            device_id_type=MESH,
        )

    def corner_copy(way):
        return pltpu.make_async_remote_copy(
            src_ref=corner_mine,
            dst_ref=corner_got[way],
            send_sem=corner_ssem.at[way],
            recv_sem=corner_rsem.at[way],
            device_id=neighbours[way],
            device_id_type=MESH,
        )

    def all_start(which, source, target, sign):
        for t in order:
            pltpu.make_async_remote_copy(
                src_ref=source.at[place(t)],
                dst_ref=target.at[place(t)],
                send_sem=all_ssem.at[which],
                recv_sem=all_rsem.at[which],
                device_id=device(t, sign),
                device_id_type=MESH,
            ).start()
        target[0] = source[0]

    def all_wait(which, source, target):
        others = pl.ds(1, count - 1)
        pltpu.make_async_remote_copy(
            src_ref=source.at[others],
            dst_ref=target.at[others],
            send_sem=all_ssem.at[which],
            recv_sem=all_rsem.at[which],
            device_id=neighbours[0],
            device_id_type=MESH,
        ).wait()

    def chunked(value):
        return value.reshape(count, WIDTH, LANES).astype(BF)

    def flat(ref):
        return ref[...].astype(F32).reshape(total, LANES)

    def part(k):
        return slice(k * LANES, (k + 1) * LANES)

    def block(f, k):
        return part(f * groups + k)

    def columns(f):
        return slice(f * face, (f + 1) * face)

    def half(side):
        return slice(2 * side * face, 2 * (side + 1) * face)

    inverse_pair = [
        [
            jnp.minimum(
                sum(j * (pair_ref[side, j] == k).astype(jnp.int32) for j in range(groups)),
                groups - 1,
            )
            for k in range(groups)
        ]
        for side in range(2)
    ]

    def met(f, k):
        return pair_ref[f // 2, k] if f in (0, 2) else k

    def slot_of(rows):
        owner = (rows * 43691) >> 22
        z = owner & (rad[3] - 1)
        x = (owner >> log2(rad[3])) & (rad[2] - 1)
        gx = owner >> log2(rad[2] * rad[3])
        c = gx & 1
        y = gx >> 1
        dy = (y - my_y + rad[0]) & (rad[0] - 1)
        dc = (c - my_c + 2) & 1
        dx = (x - my_x + rad[2]) & (rad[2] - 1)
        dz = (z - my_z + rad[3]) & (rad[3] - 1)
        return owner, rows - owner * 96, place((dy, dc, dx, dz)) * WIDTH

    block_row, offset_row, slot_row = slot_of(row_ref[...])
    wide_row[...] = jnp.full_like(wide_row, -1.0)
    wide_row[:, 0:corners] = jnp.broadcast_to(block_row.astype(F32), (wide_row.shape[0], corners))
    across = wide_row[...]
    at_col = lax.broadcasted_iota(jnp.int32, across.shape, 0)
    at_row = lax.broadcasted_iota(jnp.int32, across.shape, 1)
    earlier = (across == across.T) & (at_col < at_row)
    rank_row = jnp.sum(earlier.astype(F32), axis=0, keepdims=True)
    slot_row = slot_row + rank_row[:, 0:corners].astype(jnp.int32)
    hot = slot_row == lax.broadcasted_iota(jnp.int32, (total, corners), 0)
    offset = jnp.sum(jnp.where(hot, offset_row.astype(F32) - 200.0, 0.0), axis=1, keepdims=True)
    sent0[...] = chunked(jnp.broadcast_to(offset + 200.0, (total, LANES)))
    hot = hot.astype(F32).astype(BF)
    gather[...] = jnp.zeros_like(gather)
    gather[:, 0:corners] = hot

    coarse_pad[...] = jnp.zeros_like(coarse_pad)
    coarse_pad[0 : coarse_ref.shape[0], 0 : coarse_ref.shape[1]] = coarse_ref[...]
    slots[...] = jnp.zeros_like(slots)
    square[...] = jnp.zeros_like(square)
    for ref in (direc, image, wave, mult, owned, *lift):
        ref[...] = jnp.zeros_like(ref)
    for k in range(groups):
        halo_send[0][0][k] = load_ref[0, :, part(k)].astype(BF)
        halo_send[0][2][k] = load_ref[1, :, part(k)].astype(BF)

    pl.semaphore_wait(barrier, count - 1)
    first = [halo_copy(0, 2), halo_copy(0, 0)]
    for copy in first:
        copy.start()
    all_start(0, sent0, got0, 1)

    copies[0].wait()
    copies[1].wait()
    product = jnp.dot(couple[...], inverse[...], preferred_element_type=F32)
    for side in (1, 0):
        low, high = 2 * side, 2 * side + 1
        for k in range(groups):
            face_send[high - 1][k] = product[:, block(high, k)].astype(BF)
            face_low[k] = product[:, block(low, k)]
        for k in range(groups):
            face_send[high][k] = face_low[inverse_pair[side][k]].astype(BF)
    for f in range(4):
        for k in range(groups):
            lift[f][0:corners, part(k)] = (product[:, block(f, k)] * live[f]).astype(BF)
    spread = jnp.dot(hot, product.astype(BF), preferred_element_type=F32)
    for k in range(4 * groups):
        drop[part(k), :] = spread[:, part(k)].T.astype(BF)

    def put_resid(f, k, value):
        resid[:, block(f, k)] = value
        weights[:, block(f, k)] = (0.5 * value).astype(BF)

    def stiff_half(side, f):
        return jnp.dot(
            weights[:, half(side)], stiff[half(side), columns(f)], preferred_element_type=F32
        )

    def stiff_first():
        for f in (2, 3, 0, 1):
            out = stiff_half(0, f)
            for k in range(groups):
                values[f * groups + k] = out[:, part(k)]

    def send_faces(which, side, ways=2):
        low, high = 2 * side, 2 * side + 1
        for k in range(groups):
            if ways == 2:
                halo_send[which][high - 1][k] = values[high * groups + k].astype(BF)
            halo_send[which][high][k] = values[low * groups + inverse_pair[side][k]].astype(BF)
        sent = [halo_copy(which, way) for way in (high - 1, high)[2 - ways :]]
        for copy in sent:
            copy.start()
        return sent

    def jumped(which, f, k):
        came = halo_got[which][f][met(f, k)].astype(F32)
        return (values[f * groups + k] - came) * live[f]

    lane_slot = lax.broadcasted_iota(jnp.int32, (rhs, total), 1) & (WIDTH - 1)
    row_slot = lax.broadcasted_iota(jnp.int32, (total, LANES), 0) & (WIDTH - 1)
    real = lax.broadcasted_iota(jnp.int32, (1, LANES), 1) < rhs

    def as_row(value):
        square[0:rhs, :] = value
        return jnp.sum(square[...].T, axis=0, keepdims=True)

    def as_columns(row):
        return jnp.broadcast_to(row, (LANES, LANES)).T[0:rhs]

    def dots_row(received):
        return jnp.sum(jnp.where(row_slot == WIDTH - 1, received, 0.0), axis=0, keepdims=True)

    def setup():
        all_wait(0, sent0, got0)
        lane = lax.broadcasted_iota(jnp.int32, (total, LANES), 1).astype(F32)
        pick = (flat(got0) == lane).astype(F32).astype(BF)
        wide = jnp.dot(pick, coarse_pad[...].astype(BF), preferred_element_type=F32).astype(BF)
        solve[...] = lax.dot_general(
            wide, pick, (((1,), (1,)), ((), ())), preferred_element_type=F32
        ).astype(BF)

    def setup_faces():
        for f in range(4):
            face_copy(f).wait()
            for k in range(groups):
                came = face_got[f][met(f, k)].astype(F32) * -live[f]
                lift[f][held : held + corners, part(k)] = came.astype(BF)

    def precondition(meanwhile=None):
        sent = [None, None]
        for side in (1, 0):
            for f in (2 * side, 2 * side + 1):
                out = stiff_half(1, f)
                for k in range(groups):
                    values[f * groups + k] = values[f * groups + k] + out[:, part(k)]
            sent[side] = send_faces(1, side)
        norm = jnp.zeros((rhs, LANES), F32)
        for f in range(4):
            for k in range(groups):
                norm = norm + resid[:, block(f, k)] * values[f * groups + k]
        norm_part[...] = norm
        if meanwhile is not None:
            meanwhile()
        for side in (0, 1):
            for copy in sent[side]:
                copy.wait()
            for f in (2 * side, 2 * side + 1):
                for k in range(groups):
                    z = 0.5 * jumped(1, f, k)
                    prec[:, block(f, k)] = z
                    weights[:, block(f, k)] = z.astype(BF)
            out = jnp.dot(weights[:, half(side)], drop[half(side), :], preferred_element_type=F32)
            if side == 0:
                slots[0:rhs, :] = out
        norm_col = 0.5 * jnp.sum(norm_part[...], axis=1, keepdims=True)
        slots[0:rhs, :] = jnp.where(lane_slot == WIDTH - 1, norm_col, slots[0:rhs, :] + out)
        sent1[...] = chunked(slots[...].T)
        all_start(1, sent1, got1, 1)

    def operate(carry, step, last):
        norm_before, local_before = carry
        later = 1.0 if last else (step > 0).astype(F32)
        part_new = jnp.zeros((rhs, LANES), F32)
        part_mix = jnp.zeros((rhs, LANES), F32)
        sent = []
        for side in (1, 0):
            for f in (2 * side, 2 * side + 1):
                out = jnp.dot(weights[...], inverse[:, columns(f)], preferred_element_type=F32)
                for k in range(groups):
                    at = block(f, k)
                    v = out[:, part(k)]
                    values[f * groups + k] = v
                    part_new = part_new + prec[:, at] * v
                    part_mix = part_mix + (prec[:, at] * image[:, at] + direc[:, at] * v)
            sent += send_faces(0, side, 1 if last else 2)
        dot_new = as_row(part_new)
        dot_mix = as_row(part_mix)

        all_wait(1, sent1, got1)
        received = flat(got1)
        norm = dots_row(received)
        beta = jnp.where(real, norm / norm_before, 0.0) * later
        owned[...] = received + beta * owned[...]
        sums = owned[...]
        solved = jnp.dot(solve[...], sums.astype(BF), preferred_element_type=F32)
        local = dot_new + beta * (dot_mix + beta * local_before)
        energy = local + jnp.sum(sums * solved, axis=0, keepdims=True)
        sent2[...] = chunked(jnp.where(row_slot == WIDTH - 1, energy, solved))
        all_start(2, sent2, got2, -1)

        beta_cols = as_columns(beta)
        for f in range(4):
            for k in range(groups):
                at = block(f, k)
                direc[:, at] = prec[:, at] + beta_cols * direc[:, at]
                image[:, at] = values[f * groups + k] + beta_cols * image[:, at]
        for copy in sent:
            copy.wait()
        if not last:
            pl.when(step == 0)(setup_faces)
        needed = (1, 3) if last else (0, 1, 2, 3)
        for f in needed:
            for k in range(groups):
                at = block(f, k)
                wave[:, at] = jumped(0, f, k) + beta_cols * wave[:, at]

        all_wait(2, sent2, got2)
        received = flat(got2)
        picked = received.T[0:rhs].astype(BF)
        mine = jnp.dot(picked, gather[...], preferred_element_type=F32).astype(BF)
        corner_mine[...] = mine
        sent = [[corner_copy(f) for f in needed if f // 2 == side] for side in range(2)]
        for copy in sent[1] + sent[0]:
            copy.start()
        alpha = jnp.where(real, norm / dots_row(received), 0.0)
        alpha_cols = as_columns(alpha)
        for i, f in enumerate((1, 3)):
            for k in range(groups):
                at = part(i * groups + k)
                mult[:, at] = mult[:, at] + alpha_cols * direc[:, block(f, k)]
        for f in needed:
            own = jnp.dot(mine, lift[f][0:held, :], preferred_element_type=F32)
            for k in range(groups):
                at = block(f, k)
                whole[:, at] = wave[:, at] + own[:, part(k)]
        for side in range(2):
            for copy in sent[side]:
                copy.wait()
            for f in needed:
                if f // 2 == side:
                    other = jnp.dot(
                        corner_got[f][...], lift[f][held:, :], preferred_element_type=F32
                    )
                    for k in range(groups):
                        at = block(f, k)
                        q = whole[:, at] + other[:, part(k)]
                        put_resid(f, k, resid[:, at] - alpha_cols * q)
            if side == 0 and not last:
                stiff_first()
        return norm, local

    first[1].wait()
    for k in range(groups):
        put_resid(1, k, load_ref[0, :, part(k)] * live[1])
        put_resid(0, k, -halo_got[0][0][met(0, k)].astype(F32) * live[0])
    copies[2].wait()
    stiff_first()
    first[0].wait()
    for k in range(groups):
        put_resid(3, k, load_ref[1, :, part(k)] * live[3])
        put_resid(2, k, -halo_got[0][2][met(2, k)].astype(F32) * live[2])
    precondition(setup)
    for f in (2, 3, 0, 1):
        face_copy(f).start()

    def iteration(step, carry):
        carry = operate(carry, step, False)
        precondition()
        return carry

    carry = (jnp.ones((1, LANES), F32), jnp.zeros((1, LANES), F32))
    carry = lax.fori_loop(0, ITERS - 1, iteration, carry)
    operate(carry, ITERS - 1, True)
    for i, f in enumerate((1, 3)):
        mult_ref[i] = mult[:, columns(i)]
        res_ref[i] = resid[:, columns(f)]


def passed_on(mult_in, res_in, mult_out, res_out, mult_held, res_held, in_sem, out_sem):
    parts = [
        (ref[0].at[i], ref[1].at[i], ref[2].at[i])
        for i in range(2)
        for ref in ((mult_in, mult_held, mult_out), (res_in, res_held, res_out))
    ]
    come = [pltpu.make_async_copy(p[0], p[1], in_sem.at[i]) for i, p in enumerate(parts)]
    go = [pltpu.make_async_copy(p[1], p[2], out_sem.at[i]) for i, p in enumerate(parts)]
    for copy in come:
        copy.start()
    for i in range(4):
        come[i].wait()
        go[i].start()
    for copy in go:
        copy.wait()


def on_device(nx, ny, load, schur_inv, schur, coupling, pairing, corner_rows, coarse_inv):
    field = load[0, 0]
    rhs, face = field.shape[1:]
    width = 4 * face
    groups = face // LANES
    corners = corner_rows.shape[-1]
    total = nx * ny * WIDTH
    vmem = pl.BlockSpec(memory_space=pltpu.VMEM)
    hbm = pl.BlockSpec(memory_space=pl.ANY)
    smem = pl.BlockSpec(memory_space=pltpu.SMEM)
    held = -(-corners // 256) * 256
    corner = pltpu.VMEM((rhs, held), BF)
    halo = pltpu.VMEM((groups, rhs, LANES), BF)
    chunk = pltpu.VMEM((nx * ny, WIDTH, LANES), BF)
    state = pltpu.VMEM((rhs, width), F32)
    dma = pltpu.SemaphoreType.DMA
    out = jax.ShapeDtypeStruct(field.shape, F32)
    mult, res = pl.pallas_call(
        functools.partial(kernel, nx, ny),
        out_shape=(out, out),
        in_specs=[vmem, hbm, hbm, hbm, smem, vmem, vmem],
        out_specs=(vmem, vmem),
        scratch_shapes=[
            pltpu.VMEM((width, width), BF),
            pltpu.VMEM((width, width), BF),
            pltpu.VMEM((corners, width), BF),
            pltpu.VMEM((width, total), BF),
            pltpu.VMEM((total, total), BF),
            pltpu.VMEM((total, held), BF),
            pltpu.VMEM((LANES, LANES), F32),
            state, state, state, state, state, state,
            pltpu.VMEM((rhs, 2 * face), F32),
            pltpu.VMEM((rhs, width), BF),
            pltpu.VMEM((4 * groups, rhs, LANES), F32),
            pltpu.VMEM((rhs, LANES), F32),
            pltpu.VMEM((held, held), F32),
            pltpu.VMEM((LANES, total), F32),
            chunk, chunk, chunk, chunk, chunk, chunk,
            pltpu.VMEM((total, LANES), F32),
            pltpu.VMEM((LANES, LANES), F32),
            corner,
            pltpu.VMEM((groups, corners, LANES), F32),
            *([halo] * 16),
            *([pltpu.VMEM((groups, corners, LANES), BF)] * 8),
            *([pltpu.VMEM((2 * held, face), BF)] * 4),
            *([corner] * 4),
            dma((3,)), dma((2, 4)), dma((2, 4)), dma((3,)), dma((3,)),
            dma((4,)), dma((4,)), dma((4,)), dma((4,)),
        ],
        compiler_params=pltpu.CompilerParams(
            collective_id=0, has_side_effects=True, vmem_limit_bytes=58 * 2**20
        ),
        name="feti",
    )(
        field, schur_inv[0, 0], schur[0, 0], coupling[0, 0].T, pairing[0, 0],
        corner_rows[0], coarse_inv,
    )
    mult, res = pl.pallas_call(
        passed_on,
        out_shape=(out, out),
        in_specs=[hbm, hbm],
        out_specs=(hbm, hbm),
        scratch_shapes=[pltpu.VMEM(field.shape, F32)] * 2 + [dma((4,)), dma((4,))],
        name="passed_on",
    )(mult, res)
    return (mult[None, None], res[None, None])


def solution(mesh):
    placed = (
        P("gx", "gy", None, None, None),
        P("gx", "gy", None, None),
        P("gx", "gy", None, None),
        P("gx", "gy", None, None),
        P("gx", "gy", None, None),
        P("gx", "gy", None),
        P(("gx", "gy"), None),
    )
    return jax.shard_map(
        functools.partial(on_device, mesh.shape["gx"], mesh.shape["gy"]),
        mesh=mesh,
        in_specs=placed,
        out_specs=(P("gx", "gy", None, None, None), P("gx", "gy", None, None, None)),
        check_vma=False,
    )
```

time: 109 us -> 92.9 us (0.85)
  Pallas kernels: 101 us -> 91.9 us
  local copies, waits for them, and re-layouts: 7.31 us -> 0 us
    pallas_call x1, Pallas kernels: 101 us -> 89.9 us  [on_device(): pl.pallas_call(functools.partial(kernel, nx, ny), out_shape=(out, out), i...]
    unnamed x3 -> x0, local copies, waits for them, and re-layouts: 5.86 us -> none
    pallas_call x0 -> x1, Pallas kernels: none -> 2.04 us  [on_device(): pl.pallas_call(passed_on, out_shape=(out, out), in_specs=[hbm, hbm], out_...]
    another operation x1 -> x0, local copies, waits for them, and re-layouts: 1.44 us -> none  [on_device(): corner_rows[0, 0][:, None]]
where the time goes in v2:
time: 92.9 us; the launch traced here: 92.8 us
  Pallas kernels  91.9 us (99%)
    pallas_call x1, Pallas kernels, on_device(): pl.pallas_call(functools.partial(kernel, nx, ny), out_shape=(out, out), i...  89.9 us
    pallas_call x1, Pallas kernels, on_device(): pl.pallas_call(passed_on, out_shape=(out, out), in_specs=[hbm, hbm], out_...  2.04 us

profile of v2, /device:TPU:1, one launch (start us, length us, event | category | flops | bytes accessed | tf_op | source)
XLA Modules:
  0.0 92.8 jit_solution(7897619473437683371)
XLA Ops:
  0.6 89.9 %feti.1 = (f32[2,112,512]{2,1,0:T(8,128)}, f32[2,112,512]{2,1,0:T(8,128)}) custom-call(f32[2,112,512]{2,1,0:T(8,128)} %bitcast.13, bf16[2048,2048]{1,0:T(8,128)(2,1)} %bitcast.10, bf16[2048,2048]{1,0:T(8,128)(2,1)} %bitcast.11, bf16[192,2048]{1,0:T(8,128)(2,1)} %bitcast.12, s32[2,4]{1,0:T(2,128)} %bitcast.14, s32[1,192]{1,0:T(1,128)} %bitcast.15, ...), custom_call_target="tpu_custom_call" | custom-call | tf_op jit(solution)/shard_map/feti/pallas_call | solution.py:482
  90.6 2.0 %passed_on.1 = (f32[2,112,512]{2,1,0:T(8,128)}, f32[2,112,512]{2,1,0:T(8,128)}) custom-call(f32[2,112,512]{2,1,0:T(8,128)} %get-tuple-element.6.mult_in, f32[2,112,512]{2,1,0:T(8,128)} %get-tuple-element.7.res_in), custom_call_target="tpu_custom_call" | custom-call | tf_op jit(solution)/shard_map/passed_on/pallas_call | solution.py:522

commit v3 on v2

--- a/solution.py
+++ b/solution.py
@@ -41,7 +41,7 @@
     load_ref, inverse_hbm, stiff_hbm, couple_hbm, pair_ref, row_ref, coarse_ref,
     mult_ref, res_ref,
     inverse, stiff, couple, drop, solve, gather, coarse_pad,
-    resid, direc, image, wave, whole, prec, mult, weights, values, norm_part,
+    resid, direc, image, wave, prec, whole, mult, weights, values, norm_part,
     wide_row, slots, sent0, got0, sent1, got1, sent2, got2, owned, square, corner_mine, face_low, *rest,
 ):
     halo_send = (rest[0:4], rest[4:8])
@@ -49,7 +49,7 @@
     face_send, face_got = rest[16:20], rest[20:24]
     lift, corner_got = rest[24:28], rest[28:32]
     load_sem, halo_ssem, halo_rsem, all_ssem, all_rsem = rest[32:37]
-    face_ssem, face_rsem, corner_ssem, corner_rsem = rest[37:41]
+    face_ssem, face_rsem, corner_ssem, corner_rsem, round_sem = rest[37:42]
     rhs = load_ref.shape[1]
     face = load_ref.shape[2]
     groups = face // LANES
@@ -81,9 +81,12 @@
     for copy in copies:
         copy.start()
 
+    along_x = [(lax.rem(a + d, nx), b) for d in (1, nx - 1, *range(2, nx - 1))]
+    along_y = [(a, lax.rem(b + d, ny)) for d in (1, ny - 1, *range(2, ny - 1))]
+    along_x, along_y = along_x[: nx - 1], along_y[: ny - 1]
     barrier = pltpu.get_barrier_semaphore()
-    for t in order:
-        pl.semaphore_signal(barrier, inc=1, device_id=device(t, 1), device_id_type=MESH)
+    for peer in along_y + along_x:
+        pl.semaphore_signal(barrier, inc=1, device_id=peer, device_id_type=MESH)
 
     live = (
         (a > 0).astype(F32),
@@ -183,6 +186,17 @@
     def met(f, k):
         return pair_ref[f // 2, k] if f in (0, 2) else k
 
+    for k in range(groups):
+        halo_send[0][0][k] = load_ref[0, :, part(k)].astype(BF)
+        halo_send[0][2][k] = load_ref[1, :, part(k)].astype(BF)
+
+    pl.semaphore_wait(barrier, nx + ny - 2)
+    first = [halo_copy(0, 2), halo_copy(0, 0)]
+    for copy in first:
+        copy.start()
+    for peer in along_x:
+        pl.semaphore_signal(round_sem, inc=1, device_id=peer, device_id_type=MESH)
+
     def slot_of(rows):
         owner = (rows * 43691) >> 22
         z = owner & (rad[3] - 1)
@@ -208,9 +222,8 @@
     hot = slot_row == lax.broadcasted_iota(jnp.int32, (total, corners), 0)
     offset = jnp.sum(jnp.where(hot, offset_row.astype(F32) - 200.0, 0.0), axis=1, keepdims=True)
     sent0[...] = chunked(jnp.broadcast_to(offset + 200.0, (total, LANES)))
-    hot = hot.astype(F32).astype(BF)
     gather[...] = jnp.zeros_like(gather)
-    gather[:, 0:corners] = hot
+    gather[:, 0:corners] = hot.astype(F32).astype(BF)
 
     coarse_pad[...] = jnp.zeros_like(coarse_pad)
     coarse_pad[0 : coarse_ref.shape[0], 0 : coarse_ref.shape[1]] = coarse_ref[...]
@@ -218,16 +231,6 @@
     square[...] = jnp.zeros_like(square)
     for ref in (direc, image, wave, mult, owned, *lift):
         ref[...] = jnp.zeros_like(ref)
-    for k in range(groups):
-        halo_send[0][0][k] = load_ref[0, :, part(k)].astype(BF)
-        halo_send[0][2][k] = load_ref[1, :, part(k)].astype(BF)
-
-    pl.semaphore_wait(barrier, count - 1)
-    first = [halo_copy(0, 2), halo_copy(0, 0)]
-    for copy in first:
-        copy.start()
-    all_start(0, sent0, got0, 1)
-
     copies[0].wait()
     copies[1].wait()
     product = jnp.dot(couple[...], inverse[...], preferred_element_type=F32)
@@ -241,9 +244,12 @@
     for f in range(4):
         for k in range(groups):
             lift[f][0:corners, part(k)] = (product[:, block(f, k)] * live[f]).astype(BF)
-    spread = jnp.dot(hot, product.astype(BF), preferred_element_type=F32)
+    whole[...] = jnp.zeros_like(whole)
+    whole[0:corners, :] = product
+    scatter = gather[...].astype(F32).T.astype(BF)
     for k in range(4 * groups):
-        drop[part(k), :] = spread[:, part(k)].T.astype(BF)
+        turned = whole[:, part(k)].T.astype(BF)
+        drop[part(k), :] = jnp.dot(turned, scatter, preferred_element_type=F32).astype(BF)
 
     def put_resid(f, k, value):
         resid[:, block(f, k)] = value
@@ -289,7 +295,11 @@
     def dots_row(received):
         return jnp.sum(jnp.where(row_slot == WIDTH - 1, received, 0.0), axis=0, keepdims=True)
 
-    def setup():
+    def tell_rows():
+        pl.semaphore_wait(round_sem, nx - 1)
+        all_start(0, sent0, got0, 1)
+
+    def setup_owner():
         all_wait(0, sent0, got0)
         lane = lax.broadcasted_iota(jnp.int32, (total, LANES), 1).astype(F32)
         pick = (flat(got0) == lane).astype(F32).astype(BF)
@@ -355,6 +365,8 @@
         dot_new = as_row(part_new)
         dot_mix = as_row(part_mix)
 
+        if not last:
+            pl.when(step == 0)(setup_owner)
         all_wait(1, sent1, got1)
         received = flat(got1)
         norm = dots_row(received)
@@ -401,7 +413,7 @@
             own = jnp.dot(mine, lift[f][0:held, :], preferred_element_type=F32)
             for k in range(groups):
                 at = block(f, k)
-                whole[:, at] = wave[:, at] + own[:, part(k)]
+                whole[0:rhs, at] = wave[:, at] + own[:, part(k)]
         for side in range(2):
             for copy in sent[side]:
                 copy.wait()
@@ -412,7 +424,7 @@
                     )
                     for k in range(groups):
                         at = block(f, k)
-                        q = whole[:, at] + other[:, part(k)]
+                        q = whole[0:rhs, at] + other[:, part(k)]
                         put_resid(f, k, resid[:, at] - alpha_cols * q)
             if side == 0 and not last:
                 stiff_first()
@@ -428,7 +440,7 @@
     for k in range(groups):
         put_resid(3, k, load_ref[1, :, part(k)] * live[3])
         put_resid(2, k, -halo_got[0][2][met(2, k)].astype(F32) * live[2])
-    precondition(setup)
+    precondition(tell_rows)
     for f in (2, 3, 0, 1):
         face_copy(f).start()
 
@@ -492,7 +504,8 @@
             pltpu.VMEM((total, total), BF),
             pltpu.VMEM((total, held), BF),
             pltpu.VMEM((LANES, LANES), F32),
-            state, state, state, state, state, state,
+            state, state, state, state, state,
+            pltpu.VMEM((max(held, rhs), width), F32),
             pltpu.VMEM((rhs, 2 * face), F32),
             pltpu.VMEM((rhs, width), BF),
             pltpu.VMEM((4 * groups, rhs, LANES), F32),
@@ -510,6 +523,7 @@
             *([corner] * 4),
             dma((3,)), dma((2, 4)), dma((2, 4)), dma((3,)), dma((3,)),
             dma((4,)), dma((4,)), dma((4,)), dma((4,)),
+            pltpu.SemaphoreType.REGULAR,
         ],
         compiler_params=pltpu.CompilerParams(
             collective_id=0, has_side_effects=True, vmem_limit_bytes=58 * 2**20

time: 92.9 us -> 91.2 us (0.982)
  Pallas kernels: 91.9 us -> 90.2 us
    pallas_call x1, Pallas kernels: 89.9 us -> 88.2 us  [on_device(): pl.pallas_call(functools.partial(kernel, nx, ny), out_shape=(out, out), i...]
where the time goes in v3:
time: 91.2 us; the launch traced here: 91 us
  Pallas kernels  90.2 us (99%)
    pallas_call x1, Pallas kernels, on_device(): pl.pallas_call(functools.partial(kernel, nx, ny), out_shape=(out, out), i...  88.2 us
    pallas_call x1, Pallas kernels, on_device(): pl.pallas_call(passed_on, out_shape=(out, out), in_specs=[hbm, hbm], out_...  2.04 us

profile of v3, /device:TPU:1, one launch (start us, length us, event | category | flops | bytes accessed | tf_op | source)
XLA Modules:
  0.0 91.0 jit_solution(18003483120451881021)
XLA Ops:
  0.6 88.2 %feti.1 = (f32[2,112,512]{2,1,0:T(8,128)}, f32[2,112,512]{2,1,0:T(8,128)}) custom-call(f32[2,112,512]{2,1,0:T(8,128)} %bitcast.13, bf16[2048,2048]{1,0:T(8,128)(2,1)} %bitcast.10, bf16[2048,2048]{1,0:T(8,128)(2,1)} %bitcast.11, bf16[192,2048]{1,0:T(8,128)(2,1)} %bitcast.12, s32[2,4]{1,0:T(2,128)} %bitcast.14, s32[1,192]{1,0:T(1,128)} %bitcast.15, ...), custom_call_target="tpu_custom_call" | custom-call | tf_op jit(solution)/shard_map/feti/pallas_call | solution.py:494
  88.8 2.0 %passed_on.1 = (f32[2,112,512]{2,1,0:T(8,128)}, f32[2,112,512]{2,1,0:T(8,128)}) custom-call(f32[2,112,512]{2,1,0:T(8,128)} %get-tuple-element.6.mult_in, f32[2,112,512]{2,1,0:T(8,128)} %get-tuple-element.7.res_in), custom_call_target="tpu_custom_call" | custom-call | tf_op jit(solution)/shard_map/passed_on/pallas_call | solution.py:536

commit v4 on v3

--- a/solution.py
+++ b/solution.py
@@ -246,10 +246,8 @@
             lift[f][0:corners, part(k)] = (product[:, block(f, k)] * live[f]).astype(BF)
     whole[...] = jnp.zeros_like(whole)
     whole[0:corners, :] = product
-    scatter = gather[...].astype(F32).T.astype(BF)
-    for k in range(4 * groups):
-        turned = whole[:, part(k)].T.astype(BF)
-        drop[part(k), :] = jnp.dot(turned, scatter, preferred_element_type=F32).astype(BF)
+    pl.semaphore_wait(round_sem, nx - 1)
+    all_start(0, sent0, got0, 1)
 
     def put_resid(f, k, value):
         resid[:, block(f, k)] = value
@@ -295,11 +293,11 @@
     def dots_row(received):
         return jnp.sum(jnp.where(row_slot == WIDTH - 1, received, 0.0), axis=0, keepdims=True)
 
-    def tell_rows():
-        pl.semaphore_wait(round_sem, nx - 1)
-        all_start(0, sent0, got0, 1)
-
-    def setup_owner():
+    def setup():
+        scatter = gather[...].astype(F32).T.astype(BF)
+        for k in range(4 * groups):
+            turned = whole[:, part(k)].T.astype(BF)
+            drop[part(k), :] = jnp.dot(turned, scatter, preferred_element_type=F32).astype(BF)
         all_wait(0, sent0, got0)
         lane = lax.broadcasted_iota(jnp.int32, (total, LANES), 1).astype(F32)
         pick = (flat(got0) == lane).astype(F32).astype(BF)
@@ -365,8 +363,6 @@
         dot_new = as_row(part_new)
         dot_mix = as_row(part_mix)
 
-        if not last:
-            pl.when(step == 0)(setup_owner)
         all_wait(1, sent1, got1)
         received = flat(got1)
         norm = dots_row(received)
@@ -408,7 +404,11 @@
         for i, f in enumerate((1, 3)):
             for k in range(groups):
                 at = part(i * groups + k)
-                mult[:, at] = mult[:, at] + alpha_cols * direc[:, block(f, k)]
+                value = mult[:, at] + alpha_cols * direc[:, block(f, k)]
+                if last:
+                    mult_ref[i, :, part(k)] = value
+                else:
+                    mult[:, at] = value
         for f in needed:
             own = jnp.dot(mine, lift[f][0:held, :], preferred_element_type=F32)
             for k in range(groups):
@@ -425,7 +425,11 @@
                     for k in range(groups):
                         at = block(f, k)
                         q = whole[0:rhs, at] + other[:, part(k)]
-                        put_resid(f, k, resid[:, at] - alpha_cols * q)
+                        value = resid[:, at] - alpha_cols * q
+                        if last:
+                            res_ref[side, :, part(k)] = value
+                        else:
+                            put_resid(f, k, value)
             if side == 0 and not last:
                 stiff_first()
         return norm, local
@@ -440,7 +444,7 @@
     for k in range(groups):
         put_resid(3, k, load_ref[1, :, part(k)] * live[3])
         put_resid(2, k, -halo_got[0][2][met(2, k)].astype(F32) * live[2])
-    precondition(tell_rows)
+    precondition(setup)
     for f in (2, 3, 0, 1):
         face_copy(f).start()
 
@@ -452,9 +456,6 @@
     carry = (jnp.ones((1, LANES), F32), jnp.zeros((1, LANES), F32))
     carry = lax.fori_loop(0, ITERS - 1, iteration, carry)
     operate(carry, ITERS - 1, True)
-    for i, f in enumerate((1, 3)):
-        mult_ref[i] = mult[:, columns(i)]
-        res_ref[i] = resid[:, columns(f)]
 
 
 def passed_on(mult_in, res_in, mult_out, res_out, mult_held, res_held, in_sem, out_sem):

time: 91.2 us -> 90.9 us (level)
  no operation moved by 1% of the time
where the time goes in v4:
time: 90.9 us; the launch traced here: 90.8 us
  Pallas kernels  90 us (99%)
    pallas_call x1, Pallas kernels, on_device(): pl.pallas_call(functools.partial(kernel, nx, ny), out_shape=(out, out), i...  87.9 us
    pallas_call x1, Pallas kernels, on_device(): pl.pallas_call(passed_on, out_shape=(out, out), in_specs=[hbm, hbm], out_...  2.04 us

profile of v4, /device:TPU:1, one launch (start us, length us, event | category | flops | bytes accessed | tf_op | source)
XLA Modules:
  0.0 90.8 jit_solution(8332519258765192626)
XLA Ops:
  0.6 87.9 %feti.1 = (f32[2,112,512]{2,1,0:T(8,128)}, f32[2,112,512]{2,1,0:T(8,128)}) custom-call(f32[2,112,512]{2,1,0:T(8,128)} %bitcast.13, bf16[2048,2048]{1,0:T(8,128)(2,1)} %bitcast.10, bf16[2048,2048]{1,0:T(8,128)(2,1)} %bitcast.11, bf16[192,2048]{1,0:T(8,128)(2,1)} %bitcast.12, s32[2,4]{1,0:T(2,128)} %bitcast.14, s32[1,192]{1,0:T(1,128)} %bitcast.15, ...), custom_call_target="tpu_custom_call" | custom-call | tf_op jit(solution)/shard_map/feti/pallas_call | solution.py:495
  88.6 2.0 %passed_on.1 = (f32[2,112,512]{2,1,0:T(8,128)}, f32[2,112,512]{2,1,0:T(8,128)}) custom-call(f32[2,112,512]{2,1,0:T(8,128)} %get-tuple-element.6.mult_in, f32[2,112,512]{2,1,0:T(8,128)} %get-tuple-element.7.res_in), custom_call_target="tpu_custom_call" | custom-call | tf_op jit(solution)/shard_map/passed_on/pallas_call | solution.py:537
